TPU v7x, 128 devices: a whole 4x4x4 slice. The times are simulated.
128 devices in a mesh: tp: 4 (over y), ad: 32 (over x, z, core).
Axes of the slice: x: 4, y: 4, z: 4, core: 2. Of those that a mesh axis runs over, the one named last changes fastest.
Arguments:
- queries: bfloat16 [8192, 4096], P('ad', 'tp'), may hold values from -300 to 300
- key_cache: bfloat16 [8192, 128, 512], P('ad', None, 'tp'), may hold values from -4 to 4
- value_cache: bfloat16 [8192, 128, 512], P('ad', None, 'tp'), may hold values from -6 to 6
- new_key: bfloat16 [8192, 512], P('ad', 'tp'), may hold values from -6 to 6
- new_value: bfloat16 [8192, 512], P('ad', 'tp'), may hold values from -6 to 6
- lengths: int32 [8192], P('ad'), may hold values from 2 to 128, as said below
- out_weight: bfloat16 [4096, 8192], P('tp'), may hold values from -0.09375 to 0.09375
- shrink_weight: bfloat16 [4096, 16384], P('tp', 'ad'), may hold values from -0.09375 to 0.09375
- expand_weight: bfloat16 [16384, 8192], P('ad', 'tp'), may hold values from -0.75 to 0.75
- adapter_id: int32 [8192], P('ad'), may hold values from 0 to 255, as said below
- adapter_slot: int32 [256], replicated, may hold values from 0 to 255, as said below
Outputs:
- projected: bfloat16 [8192, 8192], P('ad', 'tp')
Inputs may be any that keep to these rules, and one draw needn't show every extreme that they name: `adapter_id`: rows are grouped by adapter within the rows of one device. Owner of adapter a is adapter_slot[a] // 8. The rows of one device name at most 16 rows for each owner, and every device names exactly 16 rows for one common owner drawn from the seed. `adapter_slot`: each value once. `lengths`: some row of every device has 128.
All inputs are finite; a program needn't handle non-finite values.
Results may differ from a plain program's by a relative error of at most 0.011.
Values may be sent and summed in bfloat16 or wider, within the bound.
A program may use at most 128 MiB of HBM per device.

v0:
```python
import math

import jax
import jax.numpy as jnp
from jax import lax
from jax.sharding import PartitionSpec as P

HEADS = 32
KV_HEADS = 4
HEAD_DIM = 128
RANK = 64


def attend(queries, key_cache, value_cache, new_key, new_value, lengths):
    row_count = queries.shape[0]
    slots = key_cache.shape[1]
    kv_local = key_cache.shape[2] // HEAD_DIM
    group = HEADS // KV_HEADS
    scale = 1.0 / math.sqrt(HEAD_DIM)
    query_four = queries.reshape(row_count, kv_local, group, HEAD_DIM)
    key_four = key_cache.reshape(row_count, slots, kv_local, HEAD_DIM)
    value_four = value_cache.reshape(row_count, slots, kv_local, HEAD_DIM)
    fresh_key = new_key.reshape(row_count, kv_local, HEAD_DIM)
    fresh_value = new_value.reshape(row_count, kv_local, HEAD_DIM).astype(jnp.float32)
    scores = (
        jnp.einsum("rkgd,rckd->rkgc", query_four, key_four, preferred_element_type=jnp.float32)
        * scale
    )
    own = (
        jnp.einsum("rkgd,rkd->rkg", query_four, fresh_key, preferred_element_type=jnp.float32)
        * scale
    )
    valid = jnp.arange(slots)[None, :] < lengths[:, None]
    valid = valid[:, None, None, :]
    scores = jnp.where(valid, scores, -jnp.inf)
    top = jnp.maximum(jnp.max(scores, axis=-1), own)
    expo = jnp.where(valid, jnp.exp(scores - top[..., None]), 0.0)
    own_expo = jnp.exp(own - top)
    total = jnp.sum(expo, axis=-1) + own_expo
    probs = (expo / total[..., None]).astype(jnp.bfloat16)
    own_prob = (own_expo / total).astype(jnp.bfloat16)
    mixed = jnp.einsum("rkgc,rckd->rkgd", probs, value_four, preferred_element_type=jnp.float32)
    mixed = mixed + own_prob.astype(jnp.float32)[..., None] * fresh_value[:, :, None, :]
    return mixed.reshape(row_count, kv_local * group * HEAD_DIM).astype(jnp.bfloat16)


def adapt(arrived, local_ids, shrink_weight, expand_weight, reduce_heads):
    owner_count, slot_count, width = arrived.shape
    flat_rows = arrived.reshape(owner_count * slot_count, width)
    flat_ids = local_ids.reshape(owner_count * slot_count)
    held = shrink_weight.shape[1] // RANK
    full_shrink = jnp.dot(flat_rows, shrink_weight, preferred_element_type=jnp.float32)
    which = jnp.arange(held * RANK, dtype=jnp.int32) // RANK
    picks = flat_ids[:, None] == which[None, :]
    partial_value = jnp.where(picks, full_shrink, 0.0).reshape(-1, held, RANK).sum(axis=1)
    shrunk = reduce_heads(partial_value).astype(jnp.bfloat16)
    spread = jnp.where(picks, jnp.tile(shrunk, (1, held)), jnp.zeros((), jnp.bfloat16))
    widened = jnp.dot(spread, expand_weight, preferred_element_type=jnp.float32).astype(
        jnp.bfloat16
    )
    return widened.reshape(owner_count, slot_count, widened.shape[1])


def shards(
    queries,
    key_cache,
    value_cache,
    new_key,
    new_value,
    lengths,
    out_weight,
    shrink_weight,
    expand_weight,
    adapter_id,
    adapter_slot,
):
    attended = attend(queries, key_cache, value_cache, new_key, new_value, lengths)
    row_count, width = attended.shape
    held = shrink_weight.shape[1] // RANK
    catalog = jnp.arange(adapter_slot.shape[0], dtype=jnp.int32)
    slot = jnp.sum(
        jnp.where(adapter_id[:, None] == catalog[None, :], adapter_slot[None, :], 0), axis=1
    )
    owner = slot // held
    local_index = slot % held
    owner_count = lax.axis_size("ad")
    capacity = 2 * row_count // owner_count
    owner_hits = (owner[:, None] == jnp.arange(owner_count, dtype=jnp.int32)[None, :]).astype(
        jnp.int32
    )
    earlier = jnp.cumsum(owner_hits, axis=0) - owner_hits
    place = owner * capacity + jnp.sum(earlier * owner_hits, axis=1)
    select = place[None, :] == jnp.arange(owner_count * capacity, dtype=jnp.int32)[:, None]
    select_matrix = select.astype(jnp.bfloat16)
    packed = jnp.dot(select_matrix, attended, preferred_element_type=jnp.float32).astype(
        jnp.bfloat16
    )
    packed = packed.reshape(owner_count, capacity, width)
    slot_index = jnp.sum(jnp.where(select, local_index[None, :], 0), axis=1).reshape(
        owner_count, capacity
    )
    arrived, local_ids = (
        lax.all_to_all(packed, "ad", split_axis=0, concat_axis=0, tiled=True),
        lax.all_to_all(slot_index, "ad", split_axis=0, concat_axis=0, tiled=True),
    )
    widened = adapt(
        arrived,
        local_ids,
        shrink_weight,
        expand_weight,
        lambda partial_value: lax.psum(partial_value, "tp"),
    )
    returned = lax.all_to_all(widened, "ad", split_axis=0, concat_axis=0, tiled=True)
    returned = returned.reshape(owner_count * capacity, returned.shape[2])
    adapted = jnp.dot(select_matrix.T, returned, preferred_element_type=jnp.float32)
    partial_base = jnp.dot(attended, out_weight, preferred_element_type=jnp.float32)
    base = lax.psum_scatter(partial_base, "tp", scatter_dimension=1, tiled=True)
    return (base + adapted).astype(jnp.bfloat16)


def solution(mesh):
    in_specs = (
        P("ad", "tp"),
        P("ad", None, "tp"),
        P("ad", None, "tp"),
        P("ad", "tp"),
        P("ad", "tp"),
        P("ad"),
        P("tp", None),
        P("tp", "ad"),
        P("ad", "tp"),
        P("ad"),
        P(),
    )
    out_specs = P("ad", "tp")
    return jax.shard_map(shards, mesh=mesh, in_specs=in_specs, out_specs=out_specs, check_vma=False)
```

profile of v0, /device:TPU:1, one launch (start us, length us, event | category | flops | bytes accessed | tf_op | source)
XLA Modules:
  0.0 150.0 jit_solution(10672959812957457667)
XLA Ops:
  6.5 1.3 copy.32
  7.8 0.8 iota_compare_fusion.4
  8.7 1.5 convert_element_type.45
  10.1 6.9 %fusion.32 = (f32[256,8]{1,0:T(8,128)S(1)}, f32[256,8,128]{2,1,0:T(8,128)S(1)}) fusion(bf16[256,8,128]{2,1,0:T(8,128)(2,1)S(1)} %bitcast.71, bf16[256,128,128]{2,1,0:T(8,128)(2,1)} %param.12, pred[256,128]{1,0:T(8,128)(4,1)S(1)} %iota_compare_fusion.4), kind=kOutput, calls=%fused_computation.71 | convolution fusion | flops 67893248 | bytes 10002432 | tf_op jit(solution)/shard_map/rkgd,rckd->rkgc/dot_general | solution.py:26
  17.1 1.5 fusion.18
  18.8 0.7 fusion.3
  19.8 0.8 copy.25
  20.6 5.7 %fusion.2 = bf16[256,8,128]{2,1,0:T(8,128)(2,1)S(1)} fusion(bf16[256,128,128]{2,1,0:T(8,128)(2,1)} %param.13, f32[256,8,128]{2,1,0:T(8,128)S(1)} %get-tuple-element.10, f32[256,128]{1,0:T(8,128)} %convert_element_type.45, f32[256,8]{1,0:T(8,128)S(1)} %copy.26, f32[256,8]{1,0:T(8,128)} %copy.25, f32[256,8]{1,0:T(8,128)S(1)} %copy.23, ...), kind=kOutput, calls=%fused_computation.9 | convolution fusion | flops 68943872 | bytes 10149888 | tf_op jit(solution)/shard_map/rkgc,rckd->rkgd/dot_general | solution.py:42
  26.3 0.8 copy-done.1
  27.1 12.5 %fusion.5 = f32[256,8192]{1,0:T(8,128)} fusion(bf16[1024,8192]{1,0:T(8,128)(2,1)} %param.17, bf16[32,8,8,128]{3,2,1,0:T(8,128)(2,1)S(1)} %bitcast.69), kind=kOutput, calls=%fused_computation.14 | convolution fusion | flops 4294967296 | bytes 25690112 | tf_op jit(solution)/shard_map/dot_general | solution.py:116
  39.6 0.6 copy-done.4
  41.5 0.7 all_to_all.12
  42.2 9.4 %all-to-all-start = ((s32[32,1,16]{2,1,0:T(1,128)}), s32[32,1,16]{2,1,0:T(1,128)S(1)}, u32[]{:S(2)}, u32[]{:S(2)}) async-start(s32[32,1,16]{2,1,0:T(1,128)} %bitcast.4), calls=%async_computation.1 | async-start | bytes 32768 | tf_op jit(solution)/shard_map/all_to_all | solution.py:104
  51.7 1.4 convolution_convert_fusion.1
  53.1 5.5 %all-to-all-done = s32[32,1,16]{2,1,0:T(1,128)S(1)} async-done(((s32[32,1,16]{2,1,0:T(1,128)}), s32[32,1,16]{2,1,0:T(1,128)S(1)}, u32[]{:S(2)}, u32[]{:S(2)}) %all-to-all-start) | async-done | bytes 2080 | tf_op jit(solution)/shard_map/all_to_all | solution.py:104
  58.6 4.2 %all-to-all-start.1 = ((bf16[32,16,1024]{2,1,0:T(8,128)(2,1)}), bf16[32,16,1024]{2,1,0:T(8,128)(2,1)S(1)}, u32[]{:S(2)}, u32[]{:S(2)}) async-start(bf16[32,16,1024]{2,1,0:T(8,128)(2,1)} %bitcast.5), calls=%async_computation.2 | async-start | bytes 2097152 | tf_op jit(solution)/shard_map/all_to_all | solution.py:103
  63.4 0.7 reduce.9
  64.2 15.6 %all-to-all-done.1 = bf16[32,16,1024]{2,1,0:T(8,128)(2,1)S(1)} async-done(((bf16[32,16,1024]{2,1,0:T(8,128)(2,1)}), bf16[32,16,1024]{2,1,0:T(8,128)(2,1)S(1)}, u32[]{:S(2)}, u32[]{:S(2)}) %all-to-all-start.1) | async-done | bytes 1048608 | tf_op jit(solution)/shard_map/all_to_all | solution.py:103
  79.9 3.0 %convolution_select_fusion = f32[512,512]{0,1:T(8,128)} fusion(bf16[512,1024]{1,0:T(8,128)(2,1)S(1)} %bitcast.74, bf16[1024,512]{1,0:T(8,128)(2,1)} %param.18, s32[512]{0:T(512)S(1)} %eq.76, s32[512]{0:T(512)S(1)} %add_select_fusion), kind=kOutput, calls=%fused_computation.7 | convolution fusion | flops 537395200 | bytes 3149824 | tf_op jit(solution)/shard_map/dot_general | solution.py:52
  82.8 1.3 reduce_sum.52
  84.1 19.2 %all-reduce.1 = bf16[512,64]{0,1:T(8,128)(2,1)S(1)} all-reduce(f32[512,64]{0,1:T(8,128)S(1)} %reduce_sum.52), channel_id=1, replica_groups=mesh['tp'=4,'ad'=32] {'tp'}, use_global_device_ids=true, to_apply=%region_9.10 | all-reduce | flops 32768 | bytes 196608 | tf_op jit(solution)/shard_map/psum | solution.py:111
  103.3 1.4 convolution_convert_fusion
  104.7 34.4 %all_to_all.19 = bf16[32,16,2048]{2,1,0:T(8,128)(2,1)} all-to-all(bf16[32,16,2048]{2,1,0:T(8,128)(2,1)S(1)} %bitcast.73), channel_id=1, replica_groups=mesh['tp'=4,'ad'=32] {'ad'}, dimensions={0} | all-to-all | bytes 4194304 | tf_op jit(solution)/shard_map/all_to_all | solution.py:113
  139.2 4.0 %fusion = bf16[256,2048]{1,0:T(8,128)(2,1)} fusion(f32[256,2048]{1,0:T(8,128)} %reduce-scatter.2.cloned.1.call-done, bf16[512,2048]{1,0:T(8,128)(2,1)} %bitcast.68, s32[256]{0:T(256)S(1)} %multiply_add_fusion), kind=kOutput, calls=%fused_computation.2 | convolution fusion | flops 538050560 | bytes 5243904 | tf_op jit(solution)/shard_map/dot_general | solution.py:115
  (37 shorter events, 2.5 us)
Async XLA Ops:
  6.5 96.8 %copy-start = (bf16[512,2048]{1,0:T(8,128)(2,1)S(1)}, bf16[512,2048]{1,0:T(8,128)(2,1)}, u32[]{:S(2)}) copy-start(bf16[512,2048]{1,0:T(8,128)(2,1)} %param.19) | copy-start | bytes 6291460
  6.5 132.6 %reduce-scatter.2.cloned.1.call-start = ((), (), s32[]{:S(2)}) async-start(), calls=%async_computation.4 | async-start | bytes 10485760 | tf_op jit(solution)/shard_map/reduce_scatter | solution.py:117
  7.8 9.2 %copy-start.3 = (bf16[32,8,8,128]{3,2,1,0:T(8,128)(2,1)}, bf16[32,8,8,128]{3,2,1,0:T(8,128)(2,1)S(1)}, u32[]{:S(2)}) copy-start(bf16[32,8,8,128]{3,2,1,0:T(8,128)(2,1)S(1)} %copy.32) | copy-start | bytes 1572868
  10.1 7.0 %copy-start.6 = (bf16[256,128]{1,0:T(8,128)(2,1)S(1)}, bf16[256,128]{1,0:T(8,128)(2,1)}, u32[]{:S(2)}) copy-start(bf16[256,128]{1,0:T(8,128)(2,1)} %param.14) | copy-start | bytes 196612
  26.3 0.8 copy-start.1
  39.5 0.7 copy-start.4
  39.5 0.7 copy-start.5
  39.5 12.1 %copy-start.2 = (bf16[256,8,128]{2,1,0:T(8,128)(2,1)S(1)}, bf16[256,8,128]{2,1,0:T(8,128)(2,1)}, u32[]{:S(2)}) copy-start(bf16[256,8,128]{2,1,0:T(8,128)(2,1)} %copy-done.1) | copy-start | bytes 1572868
  42.2 16.4 %all-to-all-start = ((s32[32,1,16]{2,1,0:T(1,128)}), s32[32,1,16]{2,1,0:T(1,128)S(1)}, u32[]{:S(2)}, u32[]{:S(2)}) async-start(s32[32,1,16]{2,1,0:T(1,128)} %bitcast.4), calls=%async_computation.1 | async-start | bytes 32768 | tf_op jit(solution)/shard_map/all_to_all | solution.py:104
  58.6 21.2 %all-to-all-start.1 = ((bf16[32,16,1024]{2,1,0:T(8,128)(2,1)}), bf16[32,16,1024]{2,1,0:T(8,128)(2,1)S(1)}, u32[]{:S(2)}, u32[]{:S(2)}) async-start(bf16[32,16,1024]{2,1,0:T(8,128)(2,1)} %bitcast.5), calls=%async_computation.2 | async-start | bytes 2097152 | tf_op jit(solution)/shard_map/all_to_all | solution.py:103
Sparse Core Ops, SparseCore 0:
  39.7 86.2 reduce-scatter.1
where the time goes:
time: 151 us; the launch traced here: 150 us
  blocking collectives  53.6 us (35%)
  matrix products  36.3 us (24%)
  waiting for transfers between devices  21.2 us (14%)
  starting transfers between devices  13.7 us (9%)
  between operations  13.6 us (9%)
  other arithmetic  6.13 us (4%)
  local copies, waits for them, and re-layouts  5.59 us (4%)
    all_to_all x1, blocking collectives, shards(): lax.all_to_all(widened, 'ad', split_axis=0, concat_axis=0, tiled=True)  34.4 us
    psum x1, blocking collectives, shards(): lax.psum(partial_value, 'tp')  19.2 us
    all_to_all x1, waiting for transfers between devices, shards(): lax.all_to_all(packed, 'ad', split_axis=0, concat_axis=0, tiled=True)  15.6 us
    dot_general x1, matrix products, shards(): jnp.dot(attended, out_weight, preferred_element_type=jnp.float32)  12.5 us
    all_to_all x1, starting transfers between devices, shards(): lax.all_to_all(slot_index, 'ad', split_axis=0, concat_axis=0, tiled=True)  9.43 us
    dot_general x1, matrix products, attend(): jnp.einsum('rkgd,rckd->rkgc', query_four, key_four, preferred_element_typ...  6.92 us
    dot_general x1, matrix products, attend(): jnp.einsum('rkgc,rckd->rkgd', probs, value_four, preferred_element_type=j...  5.72 us
    all_to_all x1, waiting for transfers between devices, shards(): lax.all_to_all(slot_index, 'ad', split_axis=0, concat_axis=0, tiled=True)  5.52 us
  transfers between devices with their start and end apart: 3, of which 2 were waited for; matrix products, arithmetic and copies ran while one was open for 6% of the time, Pallas kernels for 0%

commit v1 on v0

v1 whole, which is shorter than its diff:
```python
import math

import jax
import jax.numpy as jnp
from jax import lax
from jax.experimental import pallas as pl
from jax.experimental.pallas import tpu as pltpu
from jax.sharding import PartitionSpec as P

HEADS = 8
DIM = 128
RANK = 64
HELD = 8
ROWS = 256
SLOTS = 128
TP = 4
PEERS = 32
CAP = 16
WIDTH = HEADS * DIM
CHUNK = 2048
HALF = CHUNK // 2
AUX = 128
PACK = WIDTH + AUX
QUARTERS = 4
QPEERS = PEERS // QUARTERS
QROWS = QPEERS * CAP
KV_CHUNKS = 8
KV_ROWS = ROWS // KV_CHUNKS
BLOCK = 16
BF = jnp.bfloat16
F32 = jnp.float32
MESH = pl.DeviceIdType.MESH
NT = (((1,), (1,)), ((), ()))


def peer_offsets():
    quarters = [[] for _ in range(QUARTERS)]
    for dx in range(4):
        for dz in range(4):
            for dc in range(2):
                quarters[(dx + dz) % 2 + 2 * dc].append((dx, dz, dc))
    return [offset for quarter in quarters for offset in quarter]


OFFSETS = peer_offsets()


def iota(shape, axis):
    return lax.broadcasted_iota(jnp.int32, shape, axis)


def mm(a, b):
    return jnp.dot(a, b, preferred_element_type=F32)


def mm_nt(a, b):
    return lax.dot_general(a, b, NT, preferred_element_type=F32)


def kernel(
    q_hbm, k_hbm, v_hbm, nk_hbm, nv_hbm, w_hbm, shrink_hbm, expand_hbm, len_ref, id_ref, slot_ref,
    out_ref,
    q, kbuf, vbuf, nk, nv, wbuf, shrink, expand, qscr, oscr, att, sel, sel_t,
    packed, arrived, wid, ret, picks, ar_own, ar_send, ar_recv, rs_send, rs_recv, hold, own,
    sem_small, sem_k, sem_v, sem_w,
    s_fwd, r_fwd, s_back, r_back, s_ar, r_ar, s_rs, r_rs,
):
    me_t = lax.axis_index("tp")
    me_a = lax.axis_index("ad")
    me_x, me_z, me_c = me_a // 8, (me_a // 2) % 4, me_a % 2

    def ad_of(offset, sign):
        dx, dz, dc = offset
        x = (me_x + (sign * dx) % 4) % 4
        z = (me_z + (sign * dz) % 4) % 4
        return (x * 4 + z) * 2 + (me_c + dc) % 2

    def to_ad(offset, sign):
        return (me_t, ad_of(offset, sign))

    def to_tp(step):
        return ((me_t + step) % TP, me_a)

    def fetch(src, dst, sem):
        copy = pltpu.make_async_copy(src, dst, sem)
        copy.start()
        return copy

    small = [
        fetch(q_hbm, q, sem_small.at[0]),
        fetch(nk_hbm, nk, sem_small.at[1]),
        fetch(nv_hbm, nv, sem_small.at[2]),
    ]
    for i in range(KV_CHUNKS):
        rows = pl.ds(i * KV_ROWS, KV_ROWS)
        fetch(k_hbm.at[rows], kbuf.at[rows], sem_k.at[i])
        fetch(v_hbm.at[rows], vbuf.at[rows], sem_v.at[i])
    weights = []
    for i, step in enumerate((2, 1, 3, 0)):
        column = pl.multiple_of(((me_t + step) % TP) * CHUNK, CHUNK)
        weights.append(fetch(w_hbm.at[:, pl.ds(column, CHUNK)], wbuf.at[i], sem_w.at[i]))
        if i == 0:
            shrink_copy = fetch(shrink_hbm, shrink, sem_small.at[3])
            expand_copy = fetch(expand_hbm, expand, sem_small.at[4])

    barrier = pltpu.get_barrier_semaphore()
    for offset in OFFSETS[1:]:
        pl.semaphore_signal(barrier, inc=1, device_id=to_ad(offset, 1), device_id_type=MESH)
    for step in (1, 2, 3):
        pl.semaphore_signal(barrier, inc=1, device_id=to_tp(step), device_id_type=MESH)

    named = (iota((ROWS, ROWS), 0) == id_ref[...]).astype(F32).astype(BF)
    catalog = jnp.broadcast_to(slot_ref[...].astype(F32), (8, ROWS)).astype(BF)
    slot = mm(catalog, named)[0:1, :].astype(jnp.int32)
    owner = lax.shift_right_logical(slot, 3)
    local = jnp.bitwise_and(slot, HELD - 1)
    dx = jnp.bitwise_and(lax.shift_right_logical(owner, 3) - me_x, 3)
    dz = jnp.bitwise_and(lax.shift_right_logical(owner, 1) - me_z, 3)
    dc = jnp.bitwise_and(owner - me_c, 1)
    peer = jnp.bitwise_and(dx + dz, 1) * 8 + dc * 16 + dx * 2 + lax.shift_right_logical(dz, 1)
    hits = (iota((PEERS, ROWS), 0) == peer).astype(F32)
    before = (iota((ROWS, ROWS), 0) < iota((ROWS, ROWS), 1)).astype(F32).astype(BF)
    earlier = mm(hits.astype(BF), before)
    rank = jnp.sum(hits * earlier, axis=0, keepdims=True).astype(jnp.int32)
    place = peer * CAP + rank
    sel[...] = (iota((PEERS * CAP, ROWS), 0) == place).astype(F32).astype(BF)
    eye = (iota((ROWS, ROWS), 0) == iota((ROWS, ROWS), 1)).astype(F32).astype(BF)
    sel_t[...] = mm_nt(eye, sel[...]).astype(BF)
    local_hot = (iota((AUX, ROWS), 0) == local).astype(F32).astype(BF)
    aux = mm_nt(sel[...], local_hot).astype(BF)
    packed[:, :, WIDTH:] = aux.reshape(PEERS, CAP, AUX)

    for copy in small:
        copy.wait()
    scale = 1.0 / math.sqrt(DIM)
    group_rows = BLOCK * HEADS
    own_mask = iota((group_rows, BLOCK), 1) == iota((group_rows, BLOCK), 0) // HEADS
    lane = iota((HEADS, SLOTS), 1)
    blank = jnp.zeros((HEADS, DIM), F32)

    def attend(r0, part):
        rows = pl.ds(r0, BLOCK)
        qb = q[rows, :].astype(F32)
        for h in range(HEADS):
            qscr[part, pl.ds(h, BLOCK, stride=HEADS), :] = qb[:, h * DIM : (h + 1) * DIM]
        qv = qscr[part].astype(BF)
        fresh = mm_nt(qv, nk[rows, :]) * scale
        fresh = jnp.sum(jnp.where(own_mask, fresh, 0.0), axis=1, keepdims=True)
        pieces = []
        for i in range(BLOCK // 2):
            keys = kbuf[pl.ds(r0 + 2 * i, 2)].reshape(2 * SLOTS, DIM)
            s = mm_nt(qv[16 * i : 16 * i + 16], keys)
            for j in range(2):
                piece = s[8 * j : 8 * j + 8, SLOTS * j : SLOTS * (j + 1)] * scale
                pieces.append(jnp.where(lane < len_ref[r0 + 2 * i + j], piece, -jnp.inf))
        scores = jnp.concatenate(pieces, axis=0)
        top = jnp.maximum(jnp.max(scores, axis=1, keepdims=True), fresh)
        expo = jnp.exp(scores - top)
        fresh_expo = jnp.exp(fresh - top)
        total = jnp.sum(expo, axis=1, keepdims=True) + fresh_expo
        probs = expo / total
        fresh_prob = jnp.where(own_mask, fresh_expo / total, 0.0).astype(BF)
        mixed = []
        for i in range(BLOCK // 2):
            values = vbuf[pl.ds(r0 + 2 * i, 2)].reshape(2 * SLOTS, DIM)
            first = jnp.concatenate([probs[16 * i : 16 * i + 8], blank], axis=1)
            second = jnp.concatenate([blank, probs[16 * i + 8 : 16 * i + 16]], axis=1)
            mixed.append(mm(jnp.concatenate([first, second], axis=0).astype(BF), values))
        oscr[part] = jnp.concatenate(mixed, axis=0) + mm(fresh_prob, nv[rows, :])
        for h in range(HEADS):
            att[rows, h * DIM : (h + 1) * DIM] = oscr[part, pl.ds(h, BLOCK, stride=HEADS), :].astype(BF)

    def kv_step(i, carry):
        r0 = pl.multiple_of(i * KV_ROWS, KV_ROWS)
        rows = pl.ds(r0, KV_ROWS)
        pltpu.make_async_copy(k_hbm.at[rows], kbuf.at[rows], sem_k.at[i]).wait()
        pltpu.make_async_copy(v_hbm.at[rows], vbuf.at[rows], sem_v.at[i]).wait()
        for part in range(KV_ROWS // BLOCK):
            attend(pl.multiple_of(r0 + part * BLOCK, BLOCK), part)
        return carry

    lax.fori_loop(0, KV_CHUNKS, kv_step, 0)

    def send(src, dst, s, r, device):
        copy = pltpu.make_async_remote_copy(
            src_ref=src, dst_ref=dst, send_sem=s, recv_sem=r, device_id=device, device_id_type=MESH
        )
        copy.start()
        return copy

    packed[:, :, :WIDTH] = mm(sel[...], att[...]).astype(BF).reshape(PEERS, CAP, WIDTH)
    pl.semaphore_wait(barrier, PEERS - 1 + TP - 1)
    fwd = [None] * PEERS
    for k in range(1, PEERS):
        fwd[k] = send(packed.at[k], arrived.at[k], s_fwd.at[k], r_fwd.at[k], to_ad(OFFSETS[k], 1))
    arrived[0] = packed[0]

    tile = 512

    def ring(d, stage):
        return send(
            rs_send.at[d, stage], rs_recv.at[d, stage], s_rs.at[d, stage], r_rs.at[d, stage],
            to_tp(1 if d == 0 else 3),
        )

    def to_send(d, stage, start):
        def store(column, value):
            rs_send[d, stage, :, pl.ds(pl.multiple_of(column - start, tile), tile)] = value.astype(BF)

        return store

    def to_hold(d, start):
        def store(column, value):
            hold[d, :, pl.ds(pl.multiple_of(column - start, tile), tile)] = value

        return store

    def to_own(column, value):
        own[:, pl.ds(column, tile)] = value

    half = HALF // tile
    weights_done = [False] * TP

    def part(i, first, last, store):
        if not weights_done[i]:
            weights[i].wait()
            weights_done[i] = True

        def step(j, carry):
            column = pl.multiple_of(j * tile, tile)
            store(column, mm(att[...], wbuf[i, :, pl.ds(column, tile)]))
            return carry

        lax.fori_loop(first, last, step, 0)

    sent = [[None] * 3 for _ in range(2)]
    part(0, 0, half, to_send(0, 0, 0))
    sent[0][0] = ring(0, 0)
    part(0, half, 2 * half, to_send(1, 0, HALF))
    sent[1][0] = ring(1, 0)
    part(1, half, 2 * half, to_send(0, 1, HALF))
    part(1, 0, half, to_hold(0, 0))
    shrink_copy.wait()
    expand_copy.wait()

    spread_mask = (iota((AUX, HELD * RANK), 0) == iota((AUX, HELD * RANK), 1) // RANK).astype(F32).astype(BF)
    low = iota((QROWS // 2, 2 * RANK), 1) < RANK
    ar = [None] * QUARTERS
    back = [None] * PEERS

    def down(g):
        for k in range(g * QPEERS, (g + 1) * QPEERS):
            if k:
                fwd[k].wait_recv()
        rows = arrived[g * QPEERS : (g + 1) * QPEERS].reshape(QROWS, PACK)
        full = mm(rows[:, :WIDTH], shrink[...])
        pick = mm(rows[:, WIDTH:], spread_mask)
        picks[g] = pick.astype(BF)
        kept = jnp.where(pick > 0.5, full, 0.0)
        folded = sum(kept[:, i * 128 : (i + 1) * 128] for i in range(HELD * RANK // 128))
        both = folded + pltpu.roll(folded, RANK, 1)
        half_rows = jnp.where(low, both[: QROWS // 2], both[QROWS // 2 :])
        ar_own[g] = half_rows
        ar_send[g] = half_rows.astype(BF)
        ar[g] = [
            send(ar_send.at[g], ar_recv.at[g, d], s_ar.at[g, d], r_ar.at[g, d], to_tp(d + 1))
            for d in range(TP - 1)
        ]

    def up(g):
        for copy in ar[g]:
            copy.wait()
        total = ar_own[g]
        for d in range(TP - 1):
            total = total + ar_recv[g, d].astype(F32)
        other = pltpu.roll(total, RANK, 1)
        both = jnp.concatenate([jnp.where(low, total, other), jnp.where(low, other, total)], axis=0).astype(BF)
        spread = jnp.concatenate([both] * (HELD * RANK // 128), axis=1) * picks[g]
        peers = slice(g * QPEERS, (g + 1) * QPEERS)
        for j in range(CHUNK // tile):
            columns = slice(j * tile, (j + 1) * tile)
            wid[peers, :, columns] = mm(spread, expand[:, columns]).astype(BF).reshape(QPEERS, CAP, tile)
        for k in range(g * QPEERS, (g + 1) * QPEERS):
            if k:
                back[k] = send(wid.at[k], ret.at[k], s_back.at[k], r_back.at[k], to_ad(OFFSETS[k], -1))
            else:
                ret[0] = wid[0]

    down(0)
    part(2, 0, half, to_send(1, 1, 0))
    part(2, half, 2 * half, to_hold(1, HALF))
    down(1)
    part(3, 0, 2 * half, to_own)
    down(2)
    sent[0][1] = ring(0, 1)
    sent[1][1] = ring(1, 1)
    up(0)
    down(3)
    for d in range(2):
        sent[d][0].wait_recv()
        rs_send[d, 2] = (hold[d] + rs_recv[d, 0].astype(F32)).astype(BF)
        sent[d][2] = ring(d, 2)
    up(1)
    up(2)
    up(3)

    for d in range(2):
        sent[d][1].wait_recv()
    own[:, :HALF] += rs_recv[1, 1].astype(F32)
    own[:, HALF:] += rs_recv[0, 1].astype(F32)

    def returned(g, last=False):
        for k in range(g * QPEERS, (g + 1) * QPEERS):
            if k:
                back[k].wait_recv()
        chosen = sel_t[:, g * QROWS : (g + 1) * QROWS]
        for j in range(CHUNK // tile):
            columns = slice(j * tile, (j + 1) * tile)
            values = ret[g * QPEERS : (g + 1) * QPEERS, :, columns].reshape(QROWS, tile)
            value = own[:, columns] + mm(chosen, values)
            if last:
                out_ref[:, columns] = value.astype(BF)
            else:
                own[:, columns] = value

    returned(0)
    returned(1)
    for d in range(2):
        sent[d][2].wait_recv()
    own[:, :HALF] += rs_recv[0, 2].astype(F32)
    own[:, HALF:] += rs_recv[1, 2].astype(F32)
    returned(2)
    returned(3, last=True)

    for k in range(1, PEERS):
        fwd[k].wait_send()
        back[k].wait_send()
    for d in range(2):
        for stage in range(3):
            sent[d][stage].wait_send()


def shards(
    queries,
    key_cache,
    value_cache,
    new_key,
    new_value,
    lengths,
    out_weight,
    shrink_weight,
    expand_weight,
    adapter_id,
    adapter_slot,
):
    dma = pltpu.SemaphoreType.DMA
    hbm = pl.BlockSpec(memory_space=pl.ANY)
    vmem = pl.BlockSpec(memory_space=pltpu.VMEM)
    smem = pl.BlockSpec(memory_space=pltpu.SMEM)
    return pl.pallas_call(
        kernel,
        out_shape=jax.ShapeDtypeStruct((ROWS, CHUNK), BF),
        in_specs=[hbm] * 8 + [smem, vmem, vmem],
        out_specs=vmem,
        scratch_shapes=[
            pltpu.VMEM((ROWS, WIDTH), BF),
            pltpu.VMEM((ROWS, SLOTS, DIM), BF),
            pltpu.VMEM((ROWS, SLOTS, DIM), BF),
            pltpu.VMEM((ROWS, DIM), BF),
            pltpu.VMEM((ROWS, DIM), BF),
            pltpu.VMEM((TP, WIDTH, CHUNK), BF),
            pltpu.VMEM((WIDTH, HELD * RANK), BF),
            pltpu.VMEM((HELD * RANK, CHUNK), BF),
            pltpu.VMEM((KV_ROWS // BLOCK, BLOCK * HEADS, DIM), F32),
            pltpu.VMEM((KV_ROWS // BLOCK, BLOCK * HEADS, DIM), F32),
            pltpu.VMEM((ROWS, WIDTH), BF),
            pltpu.VMEM((PEERS * CAP, ROWS), BF),
            pltpu.VMEM((ROWS, PEERS * CAP), BF),
            pltpu.VMEM((PEERS, CAP, PACK), BF),
            pltpu.VMEM((PEERS, CAP, PACK), BF),
            pltpu.VMEM((PEERS, CAP, CHUNK), BF),
            pltpu.VMEM((PEERS, CAP, CHUNK), BF),
            pltpu.VMEM((QUARTERS, QROWS, HELD * RANK), BF),
            pltpu.VMEM((QUARTERS, QROWS // 2, 2 * RANK), F32),
            pltpu.VMEM((QUARTERS, QROWS // 2, 2 * RANK), BF),
            pltpu.VMEM((QUARTERS, TP - 1, QROWS // 2, 2 * RANK), BF),
            pltpu.VMEM((2, 3, ROWS, HALF), BF),
            pltpu.VMEM((2, 3, ROWS, HALF), BF),
            pltpu.VMEM((2, ROWS, HALF), F32),
            pltpu.VMEM((ROWS, CHUNK), F32),
            dma((5,)),
            dma((KV_CHUNKS,)),
            dma((KV_CHUNKS,)),
            dma((TP,)),
            dma((PEERS,)),
            dma((PEERS,)),
            dma((PEERS,)),
            dma((PEERS,)),
            dma((QUARTERS, TP - 1)),
            dma((QUARTERS, TP - 1)),
            dma((2, 3)),
            dma((2, 3)),
        ],
        compiler_params=pltpu.CompilerParams(
            collective_id=0, has_side_effects=True, vmem_limit_bytes=62 * 2**20
        ),
    )(
        queries,
        key_cache,
        value_cache,
        new_key,
        new_value,
        out_weight,
        shrink_weight,
        expand_weight,
        lengths,
        adapter_id.reshape(1, ROWS),
        adapter_slot.reshape(1, ROWS),
    )


def solution(mesh):
    in_specs = (
        P("ad", "tp"),
        P("ad", None, "tp"),
        P("ad", None, "tp"),
        P("ad", "tp"),
        P("ad", "tp"),
        P("ad"),
        P("tp", None),
        P("tp", "ad"),
        P("ad", "tp"),
        P("ad"),
        P(),
    )
    out_specs = P("ad", "tp")
    return jax.shard_map(shards, mesh=mesh, in_specs=in_specs, out_specs=out_specs, check_vma=False)
```

time: 151 us -> 65.9 us (0.44)
  Pallas kernels: 0 us -> 63.5 us
  blocking collectives: 53.6 us -> 0 us
  matrix products: 36.3 us -> 0 us
  waiting for transfers between devices: 21.2 us -> 0 us
  starting transfers between devices: 13.7 us -> 0 us
  between operations: 13.6 us -> 0.01 us
  other arithmetic: 6.13 us -> 0 us
  local copies, waits for them, and re-layouts: 5.59 us -> 2.3 us
    pallas_call x0 -> x1, Pallas kernels: none -> 63.5 us  [shards(): pl.pallas_call(kernel, out_shape=jax.ShapeDtypeStruct((ROWS, CHUNK), BF),...]
    dot_general x8 -> x0, matrix products: 36.3 us -> none  [the longest x1 12.5 us: shards(): jnp.dot(attended, out_weight, preferred_element_type=jnp.float32)]
    all_to_all x1 -> x0, blocking collectives: 34.4 us -> none  [shards(): lax.all_to_all(widened, 'ad', split_axis=0, concat_axis=0, tiled=True)]
    all_to_all x2 -> x0, waiting for transfers between devices: 21.1 us -> none  [the longest x1 15.6 us: shards(): lax.all_to_all(packed, 'ad', split_axis=0, concat_axis=0, tiled=True)]
    psum x1 -> x0, blocking collectives: 19.2 us -> none  [shards(): lax.psum(partial_value, 'tp')]
    all_to_all x2 -> x0, starting transfers between devices: 13.7 us -> none  [the longest x1 9.43 us: shards(): lax.all_to_all(slot_index, 'ad', split_axis=0, concat_axis=0, tiled=True)]
    reduce_sum x5 -> x0, other arithmetic: 2.43 us -> none  [the longest x1 1.31 us: adapt(): jnp.where(picks, full_shrink, 0.0).reshape(-1, held, RANK).sum(axis=1)]
  transfers between devices with their start and end apart: 3 -> 0, of which waited for: 2 -> 0; matrix products, arithmetic and copies ran while one was open for 6% -> 0% of each run, Pallas kernels for 0% -> 0%
where the time goes in v1:
time: 65.9 us; the launch traced here: 65.8 us
  Pallas kernels  63.5 us (96%)
  local copies, waits for them, and re-layouts  2.3 us (3%)
    pallas_call x1, Pallas kernels, shards(): pl.pallas_call(kernel, out_shape=jax.ShapeDtypeStruct((ROWS, CHUNK), BF),...  63.5 us
    unnamed x1, local copies, waits for them, and re-layouts  2.3 us

profile of v1, /device:TPU:1, one launch (start us, length us, event | category | flops | bytes accessed | tf_op | source)
XLA Modules:
  0.0 65.8 jit_solution(6774494720300194841)
XLA Ops:
  0.0 63.5 %shard_map.109 = bf16[256,2048]{1,0:T(8,128)(2,1)} custom-call(bf16[256,1024]{1,0:T(8,128)(2,1)} %q_hbm.1, bf16[256,128,128]{2,1,0:T(8,128)(2,1)} %k_hbm.1, bf16[256,128,128]{2,1,0:T(8,128)(2,1)} %v_hbm.1, bf16[256,128]{1,0:T(8,128)(2,1)} %nk_hbm.1, bf16[256,128]{1,0:T(8,128)(2,1)} %nv_hbm.1, bf16[1024,8192]{1,0:T(8,128)(2,1)} %w_hbm.1, ...), custom_call_target="tpu_custom_call" | custom-call | tf_op jit(solution)/shard_map/pallas_call | solution.py:360
  63.5 2.3 %copy.13 = bf16[256,2048]{1,0:T(8,128)(2,1)} copy(bf16[256,2048]{1,0:T(8,128)(2,1)} %shard_map.109) | data formatting | bytes 2097152

commit v2 on v1

--- a/solution.py
+++ b/solution.py
@@ -20,12 +20,13 @@
 CHUNK = 2048
 HALF = CHUNK // 2
 AUX = 128
-PACK = WIDTH + AUX
 QUARTERS = 4
 QPEERS = PEERS // QUARTERS
 QROWS = QPEERS * CAP
 KV_CHUNKS = 8
 KV_ROWS = ROWS // KV_CHUNKS
+KV_AHEAD = 2
+W_AFTER = 1
 BLOCK = 16
 BF = jnp.bfloat16
 F32 = jnp.float32
@@ -58,12 +59,13 @@
 
 
 def kernel(
-    q_hbm, k_hbm, v_hbm, nk_hbm, nv_hbm, w_hbm, shrink_hbm, expand_hbm, len_ref, id_ref, slot_ref,
+    q_hbm, k_hbm, v_hbm, nk_hbm, nv_hbm, w_hbm, shrink_hbm, expand_hbm, len_hbm, id_hbm, slot_hbm,
     out_ref,
+    len_ref, id_ref, slot_ref,
     q, kbuf, vbuf, nk, nv, wbuf, shrink, expand, qscr, oscr, att, sel, sel_t,
-    packed, arrived, wid, ret, picks, ar_own, ar_send, ar_recv, rs_send, rs_recv, hold, own,
+    packed, arrived, aux_send, aux_recv, wid, ret, picks, ar_own, ar_send, ar_recv, rs_send, rs_recv, hold, own,
     sem_small, sem_k, sem_v, sem_w,
-    s_fwd, r_fwd, s_back, r_back, s_ar, r_ar, s_rs, r_rs,
+    s_fwd, r_fwd, s_back, r_back, s_ar, r_ar, s_rs, r_rs, s_aux, r_aux,
 ):
     me_t = lax.axis_index("tp")
     me_a = lax.axis_index("ad")
@@ -86,22 +88,35 @@
         copy.start()
         return copy
 
+    named_copies = [fetch(id_hbm, id_ref, sem_small.at[5]), fetch(slot_hbm, slot_ref, sem_small.at[6])]
     small = [
+        fetch(len_hbm, len_ref, sem_small.at[7]),
         fetch(q_hbm, q, sem_small.at[0]),
         fetch(nk_hbm, nk, sem_small.at[1]),
         fetch(nv_hbm, nv, sem_small.at[2]),
     ]
-    for i in range(KV_CHUNKS):
-        rows = pl.ds(i * KV_ROWS, KV_ROWS)
-        fetch(k_hbm.at[rows], kbuf.at[rows], sem_k.at[i])
-        fetch(v_hbm.at[rows], vbuf.at[rows], sem_v.at[i])
-    weights = []
-    for i, step in enumerate((2, 1, 3, 0)):
-        column = pl.multiple_of(((me_t + step) % TP) * CHUNK, CHUNK)
-        weights.append(fetch(w_hbm.at[:, pl.ds(column, CHUNK)], wbuf.at[i], sem_w.at[i]))
-        if i == 0:
-            shrink_copy = fetch(shrink_hbm, shrink, sem_small.at[3])
-            expand_copy = fetch(expand_hbm, expand, sem_small.at[4])
+
+    def kv_copies(i):
+        rows = pl.ds(pl.multiple_of(i * KV_ROWS, KV_ROWS), KV_ROWS)
+        return (
+            pltpu.make_async_copy(k_hbm.at[rows], kbuf.at[rows], sem_k.at[i]),
+            pltpu.make_async_copy(v_hbm.at[rows], vbuf.at[rows], sem_v.at[i]),
+        )
+
+    def start_kv(i):
+        for copy in kv_copies(i):
+            copy.start()
+
+    for i in range(KV_AHEAD):
+        start_kv(i)
+
+    def weight_copy(i):
+        column = pl.multiple_of(((me_t + (2, 1, 3, 0)[i]) % TP) * CHUNK, CHUNK)
+        return pltpu.make_async_copy(w_hbm.at[:, pl.ds(column, CHUNK)], wbuf.at[i], sem_w.at[i])
+
+    weights = [weight_copy(i) for i in range(TP)]
+    shrink_copy = pltpu.make_async_copy(shrink_hbm, shrink, sem_small.at[3])
+    expand_copy = pltpu.make_async_copy(expand_hbm, expand, sem_small.at[4])
 
     barrier = pltpu.get_barrier_semaphore()
     for offset in OFFSETS[1:]:
@@ -109,6 +124,8 @@
     for step in (1, 2, 3):
         pl.semaphore_signal(barrier, inc=1, device_id=to_tp(step), device_id_type=MESH)
 
+    for copy in named_copies:
+        copy.wait()
     named = (iota((ROWS, ROWS), 0) == id_ref[...]).astype(F32).astype(BF)
     catalog = jnp.broadcast_to(slot_ref[...].astype(F32), (8, ROWS)).astype(BF)
     slot = mm(catalog, named)[0:1, :].astype(jnp.int32)
@@ -128,7 +145,7 @@
     sel_t[...] = mm_nt(eye, sel[...]).astype(BF)
     local_hot = (iota((AUX, ROWS), 0) == local).astype(F32).astype(BF)
     aux = mm_nt(sel[...], local_hot).astype(BF)
-    packed[:, :, WIDTH:] = aux.reshape(PEERS, CAP, AUX)
+    aux_send[...] = aux.reshape(PEERS, CAP, AUX)
 
     for copy in small:
         copy.wait()
@@ -170,17 +187,6 @@
         for h in range(HEADS):
             att[rows, h * DIM : (h + 1) * DIM] = oscr[part, pl.ds(h, BLOCK, stride=HEADS), :].astype(BF)
 
-    def kv_step(i, carry):
-        r0 = pl.multiple_of(i * KV_ROWS, KV_ROWS)
-        rows = pl.ds(r0, KV_ROWS)
-        pltpu.make_async_copy(k_hbm.at[rows], kbuf.at[rows], sem_k.at[i]).wait()
-        pltpu.make_async_copy(v_hbm.at[rows], vbuf.at[rows], sem_v.at[i]).wait()
-        for part in range(KV_ROWS // BLOCK):
-            attend(pl.multiple_of(r0 + part * BLOCK, BLOCK), part)
-        return carry
-
-    lax.fori_loop(0, KV_CHUNKS, kv_step, 0)
-
     def send(src, dst, s, r, device):
         copy = pltpu.make_async_remote_copy(
             src_ref=src, dst_ref=dst, send_sem=s, recv_sem=r, device_id=device, device_id_type=MESH
@@ -188,13 +194,6 @@
         copy.start()
         return copy
 
-    packed[:, :, :WIDTH] = mm(sel[...], att[...]).astype(BF).reshape(PEERS, CAP, WIDTH)
-    pl.semaphore_wait(barrier, PEERS - 1 + TP - 1)
-    fwd = [None] * PEERS
-    for k in range(1, PEERS):
-        fwd[k] = send(packed.at[k], arrived.at[k], s_fwd.at[k], r_fwd.at[k], to_ad(OFFSETS[k], 1))
-    arrived[0] = packed[0]
-
     tile = 512
 
     def ring(d, stage):
@@ -234,10 +233,69 @@
         lax.fori_loop(first, last, step, 0)
 
     sent = [[None] * 3 for _ in range(2)]
-    part(0, 0, half, to_send(0, 0, 0))
-    sent[0][0] = ring(0, 0)
-    part(0, half, 2 * half, to_send(1, 0, HALF))
-    sent[1][0] = ring(1, 0)
+    sent_half = [None, None]
+
+    def ring_half(d, part_of):
+        rows = pl.ds(part_of * (ROWS // 2), ROWS // 2)
+        slot_of = 0 if part_of else 3
+        return send(
+            rs_send.at[d, 0, rows], rs_recv.at[d, 0, rows], s_rs.at[d, slot_of], r_rs.at[d, slot_of],
+            to_tp(1 if d == 0 else 3),
+        )
+
+    def opposite(part_of):
+        if part_of == 0:
+            weights[0].wait()
+        rows = slice(part_of * (ROWS // 2), (part_of + 1) * (ROWS // 2))
+        for d in range(2):
+            for j in range(half):
+                columns = slice(j * tile, (j + 1) * tile)
+                value = mm(att[rows, :], wbuf[0, :, d * HALF + j * tile : d * HALF + (j + 1) * tile])
+                rs_send[d, 0, rows, columns] = value.astype(BF)
+            copy = ring_half(d, part_of)
+            if part_of:
+                sent[d][0] = copy
+            else:
+                sent_half[d] = copy
+
+    def kv_step(i, carry):
+        for copy in kv_copies(i):
+            copy.wait()
+
+        @pl.when(i < KV_CHUNKS - KV_AHEAD)
+        def _():
+            start_kv(i + KV_AHEAD)
+
+        @pl.when(i == W_AFTER)
+        def _():
+            weights[0].start()
+
+        r0 = pl.multiple_of(i * KV_ROWS, KV_ROWS)
+        for part in range(KV_ROWS // BLOCK):
+            attend(pl.multiple_of(r0 + part * BLOCK, BLOCK), part)
+        return carry
+
+    lax.fori_loop(0, KV_CHUNKS // 2, kv_step, 0)
+    pl.semaphore_wait(barrier, PEERS - 1 + TP - 1)
+    aux_sent = [None] * PEERS
+    for k in range(1, PEERS):
+        aux_sent[k] = send(aux_send.at[k], aux_recv.at[k], s_aux.at[k], r_aux.at[k], to_ad(OFFSETS[k], 1))
+    aux_recv[0] = aux_send[0]
+    opposite(0)
+    lax.fori_loop(KV_CHUNKS // 2, KV_CHUNKS, kv_step, 0)
+
+    packed[...] = mm(sel[...], att[...]).astype(BF).reshape(PEERS, CAP, WIDTH)
+    fwd = [None] * PEERS
+    for k in range(1, PEERS):
+        fwd[k] = send(packed.at[k], arrived.at[k], s_fwd.at[k], r_fwd.at[k], to_ad(OFFSETS[k], 1))
+    weights[1].start()
+    shrink_copy.start()
+    arrived[0] = packed[0]
+
+    opposite(1)
+    weights[2].start()
+    expand_copy.start()
+    weights[3].start()
     part(1, half, 2 * half, to_send(0, 1, HALF))
     part(1, 0, half, to_hold(0, 0))
     shrink_copy.wait()
@@ -251,10 +309,11 @@
     def down(g):
         for k in range(g * QPEERS, (g + 1) * QPEERS):
             if k:
+                aux_sent[k].wait_recv()
                 fwd[k].wait_recv()
-        rows = arrived[g * QPEERS : (g + 1) * QPEERS].reshape(QROWS, PACK)
-        full = mm(rows[:, :WIDTH], shrink[...])
-        pick = mm(rows[:, WIDTH:], spread_mask)
+        rows = arrived[g * QPEERS : (g + 1) * QPEERS].reshape(QROWS, WIDTH)
+        full = mm(rows, shrink[...])
+        pick = mm(aux_recv[g * QPEERS : (g + 1) * QPEERS].reshape(QROWS, AUX), spread_mask)
         picks[g] = pick.astype(BF)
         kept = jnp.where(pick > 0.5, full, 0.0)
         folded = sum(kept[:, i * 128 : (i + 1) * 128] for i in range(HELD * RANK // 128))
@@ -297,6 +356,7 @@
     up(0)
     down(3)
     for d in range(2):
+        sent_half[d].wait_recv()
         sent[d][0].wait_recv()
         rs_send[d, 2] = (hold[d] + rs_recv[d, 0].astype(F32)).astype(BF)
         sent[d][2] = ring(d, 2)
@@ -333,9 +393,11 @@
     returned(3, last=True)
 
     for k in range(1, PEERS):
+        aux_sent[k].wait_send()
         fwd[k].wait_send()
         back[k].wait_send()
     for d in range(2):
+        sent_half[d].wait_send()
         for stage in range(3):
             sent[d][stage].wait_send()
 
@@ -356,13 +418,15 @@
     dma = pltpu.SemaphoreType.DMA
     hbm = pl.BlockSpec(memory_space=pl.ANY)
     vmem = pl.BlockSpec(memory_space=pltpu.VMEM)
-    smem = pl.BlockSpec(memory_space=pltpu.SMEM)
     return pl.pallas_call(
         kernel,
-        out_shape=jax.ShapeDtypeStruct((ROWS, CHUNK), BF),
-        in_specs=[hbm] * 8 + [smem, vmem, vmem],
+        out_shape=pltpu.VMEM((ROWS, CHUNK), BF),
+        in_specs=[hbm] * 11,
         out_specs=vmem,
         scratch_shapes=[
+            pltpu.SMEM((ROWS,), jnp.int32),
+            pltpu.VMEM((1, ROWS), jnp.int32),
+            pltpu.VMEM((1, ROWS), jnp.int32),
             pltpu.VMEM((ROWS, WIDTH), BF),
             pltpu.VMEM((ROWS, SLOTS, DIM), BF),
             pltpu.VMEM((ROWS, SLOTS, DIM), BF),
@@ -376,8 +440,10 @@
             pltpu.VMEM((ROWS, WIDTH), BF),
             pltpu.VMEM((PEERS * CAP, ROWS), BF),
             pltpu.VMEM((ROWS, PEERS * CAP), BF),
-            pltpu.VMEM((PEERS, CAP, PACK), BF),
-            pltpu.VMEM((PEERS, CAP, PACK), BF),
+            pltpu.VMEM((PEERS, CAP, WIDTH), BF),
+            pltpu.VMEM((PEERS, CAP, WIDTH), BF),
+            pltpu.VMEM((PEERS, CAP, AUX), BF),
+            pltpu.VMEM((PEERS, CAP, AUX), BF),
             pltpu.VMEM((PEERS, CAP, CHUNK), BF),
             pltpu.VMEM((PEERS, CAP, CHUNK), BF),
             pltpu.VMEM((QUARTERS, QROWS, HELD * RANK), BF),
@@ -388,7 +454,7 @@
             pltpu.VMEM((2, 3, ROWS, HALF), BF),
             pltpu.VMEM((2, ROWS, HALF), F32),
             pltpu.VMEM((ROWS, CHUNK), F32),
-            dma((5,)),
+            dma((8,)),
             dma((KV_CHUNKS,)),
             dma((KV_CHUNKS,)),
             dma((TP,)),
@@ -398,11 +464,13 @@
             dma((PEERS,)),
             dma((QUARTERS, TP - 1)),
             dma((QUARTERS, TP - 1)),
-            dma((2, 3)),
-            dma((2, 3)),
+            dma((2, 4)),
+            dma((2, 4)),
+            dma((PEERS,)),
+            dma((PEERS,)),
         ],
         compiler_params=pltpu.CompilerParams(
-            collective_id=0, has_side_effects=True, vmem_limit_bytes=62 * 2**20
+            collective_id=0, has_side_effects=True, vmem_limit_bytes=58 * 2**20
         ),
     )(
         queries,

time: 65.9 us -> 61 us (0.926)
  Pallas kernels: 63.5 us -> 59.9 us
  local copies, waits for them, and re-layouts: 2.3 us -> 0.97 us
    pallas_call x1, Pallas kernels: 63.5 us -> 59.9 us  [shards(): pl.pallas_call(kernel, out_shape=pltpu.VMEM((ROWS, CHUNK), BF), in_specs=...]
    unnamed x1, local copies, waits for them, and re-layouts: 2.3 us -> 0.97 us
where the time goes in v2:
time: 61 us; the launch traced here: 60.9 us
  Pallas kernels  59.9 us (98%)
  local copies, waits for them, and re-layouts  0.97 us (2%)
    pallas_call x1, Pallas kernels, shards(): pl.pallas_call(kernel, out_shape=pltpu.VMEM((ROWS, CHUNK), BF), in_specs=...  59.9 us

profile of v2, /device:TPU:1, one launch (start us, length us, event | category | flops | bytes accessed | tf_op | source)
XLA Modules:
  0.0 60.9 jit_solution(8094371482491555324)
XLA Ops:
  0.0 59.9 %shard_map.109 = bf16[256,2048]{1,0:T(8,128)(2,1)S(1)} custom-call(bf16[256,1024]{1,0:T(8,128)(2,1)} %q_hbm.1, bf16[256,128,128]{2,1,0:T(8,128)(2,1)} %k_hbm.1, bf16[256,128,128]{2,1,0:T(8,128)(2,1)} %v_hbm.1, bf16[256,128]{1,0:T(8,128)(2,1)} %nk_hbm.1, bf16[256,128]{1,0:T(8,128)(2,1)} %nv_hbm.1, bf16[1024,8192]{1,0:T(8,128)(2,1)} %w_hbm.1, ...), custom_call_target="tpu_custom_call" | custom-call | tf_op jit(solution)/shard_map/pallas_call | solution.py:421
  59.9 1.0 %copy.13 = bf16[256,2048]{1,0:T(8,128)(2,1)} copy(bf16[256,2048]{1,0:T(8,128)(2,1)S(1)} %shard_map.109) | data formatting | bytes 2097152

commit v3 on v2

--- a/solution.py
+++ b/solution.py
@@ -44,6 +44,7 @@
 
 
 OFFSETS = peer_offsets()
+ORDER = (5, 2, 6, 1, 7, 3, 4, 0)
 
 
 def iota(shape, axis):
@@ -270,6 +271,10 @@
         def _():
             weights[0].start()
 
+        @pl.when(i == KV_CHUNKS - KV_AHEAD)
+        def _():
+            shrink_copy.start()
+
         r0 = pl.multiple_of(i * KV_ROWS, KV_ROWS)
         for part in range(KV_ROWS // BLOCK):
             attend(pl.multiple_of(r0 + part * BLOCK, BLOCK), part)
@@ -286,10 +291,11 @@
 
     packed[...] = mm(sel[...], att[...]).astype(BF).reshape(PEERS, CAP, WIDTH)
     fwd = [None] * PEERS
-    for k in range(1, PEERS):
+    for k in [q * QPEERS + j for q in range(QUARTERS) for j in ORDER][:PEERS]:
+        if k == 0:
+            continue
         fwd[k] = send(packed.at[k], arrived.at[k], s_fwd.at[k], r_fwd.at[k], to_ad(OFFSETS[k], 1))
     weights[1].start()
-    shrink_copy.start()
     arrived[0] = packed[0]
 
     opposite(1)
@@ -349,18 +355,18 @@
     part(2, 0, half, to_send(1, 1, 0))
     part(2, half, 2 * half, to_hold(1, HALF))
     down(1)
+    sent[0][1] = ring(0, 1)
+    sent[1][1] = ring(1, 1)
     part(3, 0, 2 * half, to_own)
     down(2)
-    sent[0][1] = ring(0, 1)
-    sent[1][1] = ring(1, 1)
     up(0)
+    up(1)
     down(3)
     for d in range(2):
         sent_half[d].wait_recv()
         sent[d][0].wait_recv()
         rs_send[d, 2] = (hold[d] + rs_recv[d, 0].astype(F32)).astype(BF)
         sent[d][2] = ring(d, 2)
-    up(1)
     up(2)
     up(3)
 

time: 61 us -> 58.9 us (0.966)
  Pallas kernels: 59.9 us -> 57.8 us
    pallas_call x1, Pallas kernels: 59.9 us -> 57.8 us  [shards(): pl.pallas_call(kernel, out_shape=pltpu.VMEM((ROWS, CHUNK), BF), in_specs=...]
where the time goes in v3:
time: 58.9 us; the launch traced here: 58.8 us
  Pallas kernels  57.8 us (98%)
  local copies, waits for them, and re-layouts  0.97 us (2%)
    pallas_call x1, Pallas kernels, shards(): pl.pallas_call(kernel, out_shape=pltpu.VMEM((ROWS, CHUNK), BF), in_specs=...  57.8 us

profile of v3, /device:TPU:1, one launch (start us, length us, event | category | flops | bytes accessed | tf_op | source)
XLA Modules:
  0.0 58.8 jit_solution(2743701605761094541)
XLA Ops:
  0.0 57.8 %shard_map.109 = bf16[256,2048]{1,0:T(8,128)(2,1)S(1)} custom-call(bf16[256,1024]{1,0:T(8,128)(2,1)} %q_hbm.1, bf16[256,128,128]{2,1,0:T(8,128)(2,1)} %k_hbm.1, bf16[256,128,128]{2,1,0:T(8,128)(2,1)} %v_hbm.1, bf16[256,128]{1,0:T(8,128)(2,1)} %nk_hbm.1, bf16[256,128]{1,0:T(8,128)(2,1)} %nv_hbm.1, bf16[1024,8192]{1,0:T(8,128)(2,1)} %w_hbm.1, ...), custom_call_target="tpu_custom_call" | custom-call | tf_op jit(solution)/shard_map/pallas_call | solution.py:427
  57.8 1.0 %copy.13 = bf16[256,2048]{1,0:T(8,128)(2,1)} copy(bf16[256,2048]{1,0:T(8,128)(2,1)S(1)} %shard_map.109) | data formatting | bytes 2097152

commit v4 on v3

--- a/solution.py
+++ b/solution.py
@@ -20,6 +20,7 @@
 CHUNK = 2048
 HALF = CHUNK // 2
 AUX = 128
+PACK = WIDTH + AUX
 QUARTERS = 4
 QPEERS = PEERS // QUARTERS
 QROWS = QPEERS * CAP
@@ -64,9 +65,9 @@
     out_ref,
     len_ref, id_ref, slot_ref,
     q, kbuf, vbuf, nk, nv, wbuf, shrink, expand, qscr, oscr, att, sel, sel_t,
-    packed, arrived, aux_send, aux_recv, wid, ret, picks, ar_own, ar_send, ar_recv, rs_send, rs_recv, hold, own,
+    packed, arrived, wid, ret, picks, ar_own, ar_send, ar_recv, rs_send, rs_recv, hold, own,
     sem_small, sem_k, sem_v, sem_w,
-    s_fwd, r_fwd, s_back, r_back, s_ar, r_ar, s_rs, r_rs, s_aux, r_aux,
+    s_fwd, r_fwd, s_back, r_back, s_ar, r_ar, s_rs, r_rs,
 ):
     me_t = lax.axis_index("tp")
     me_a = lax.axis_index("ad")
@@ -146,7 +147,7 @@
     sel_t[...] = mm_nt(eye, sel[...]).astype(BF)
     local_hot = (iota((AUX, ROWS), 0) == local).astype(F32).astype(BF)
     aux = mm_nt(sel[...], local_hot).astype(BF)
-    aux_send[...] = aux.reshape(PEERS, CAP, AUX)
+    packed[:, :, WIDTH:] = aux.reshape(PEERS, CAP, AUX)
 
     for copy in small:
         copy.wait()
@@ -282,14 +283,10 @@
 
     lax.fori_loop(0, KV_CHUNKS // 2, kv_step, 0)
     pl.semaphore_wait(barrier, PEERS - 1 + TP - 1)
-    aux_sent = [None] * PEERS
-    for k in range(1, PEERS):
-        aux_sent[k] = send(aux_send.at[k], aux_recv.at[k], s_aux.at[k], r_aux.at[k], to_ad(OFFSETS[k], 1))
-    aux_recv[0] = aux_send[0]
     opposite(0)
     lax.fori_loop(KV_CHUNKS // 2, KV_CHUNKS, kv_step, 0)
 
-    packed[...] = mm(sel[...], att[...]).astype(BF).reshape(PEERS, CAP, WIDTH)
+    packed[:, :, :WIDTH] = mm(sel[...], att[...]).astype(BF).reshape(PEERS, CAP, WIDTH)
     fwd = [None] * PEERS
     for k in [q * QPEERS + j for q in range(QUARTERS) for j in ORDER][:PEERS]:
         if k == 0:
@@ -315,11 +312,10 @@
     def down(g):
         for k in range(g * QPEERS, (g + 1) * QPEERS):
             if k:
-                aux_sent[k].wait_recv()
                 fwd[k].wait_recv()
-        rows = arrived[g * QPEERS : (g + 1) * QPEERS].reshape(QROWS, WIDTH)
-        full = mm(rows, shrink[...])
-        pick = mm(aux_recv[g * QPEERS : (g + 1) * QPEERS].reshape(QROWS, AUX), spread_mask)
+        rows = arrived[g * QPEERS : (g + 1) * QPEERS].reshape(QROWS, PACK)
+        full = mm(rows[:, :WIDTH], shrink[...])
+        pick = mm(rows[:, WIDTH:], spread_mask)
         picks[g] = pick.astype(BF)
         kept = jnp.where(pick > 0.5, full, 0.0)
         folded = sum(kept[:, i * 128 : (i + 1) * 128] for i in range(HELD * RANK // 128))
@@ -399,7 +395,6 @@
     returned(3, last=True)
 
     for k in range(1, PEERS):
-        aux_sent[k].wait_send()
         fwd[k].wait_send()
         back[k].wait_send()
     for d in range(2):
@@ -446,10 +441,8 @@
             pltpu.VMEM((ROWS, WIDTH), BF),
             pltpu.VMEM((PEERS * CAP, ROWS), BF),
             pltpu.VMEM((ROWS, PEERS * CAP), BF),
-            pltpu.VMEM((PEERS, CAP, WIDTH), BF),
-            pltpu.VMEM((PEERS, CAP, WIDTH), BF),
-            pltpu.VMEM((PEERS, CAP, AUX), BF),
-            pltpu.VMEM((PEERS, CAP, AUX), BF),
+            pltpu.VMEM((PEERS, CAP, PACK), BF),
+            pltpu.VMEM((PEERS, CAP, PACK), BF),
             pltpu.VMEM((PEERS, CAP, CHUNK), BF),
             pltpu.VMEM((PEERS, CAP, CHUNK), BF),
             pltpu.VMEM((QUARTERS, QROWS, HELD * RANK), BF),
@@ -472,8 +465,6 @@
             dma((QUARTERS, TP - 1)),
             dma((2, 4)),
             dma((2, 4)),
-            dma((PEERS,)),
-            dma((PEERS,)),
         ],
         compiler_params=pltpu.CompilerParams(
             collective_id=0, has_side_effects=True, vmem_limit_bytes=58 * 2**20

time: 58.9 us -> 58.6 us (level)
  no operation moved by 1% of the time
where the time goes in v4:
time: 58.6 us; the launch traced here: 58.5 us
  Pallas kernels  57.5 us (98%)
  local copies, waits for them, and re-layouts  0.97 us (2%)
    pallas_call x1, Pallas kernels, shards(): pl.pallas_call(kernel, out_shape=pltpu.VMEM((ROWS, CHUNK), BF), in_specs=...  57.5 us

profile of v4, /device:TPU:1, one launch (start us, length us, event | category | flops | bytes accessed | tf_op | source)
XLA Modules:
  0.0 58.5 jit_solution(15893167825322790115)
XLA Ops:
  0.0 57.5 %shard_map.109 = bf16[256,2048]{1,0:T(8,128)(2,1)S(1)} custom-call(bf16[256,1024]{1,0:T(8,128)(2,1)} %q_hbm.1, bf16[256,128,128]{2,1,0:T(8,128)(2,1)} %k_hbm.1, bf16[256,128,128]{2,1,0:T(8,128)(2,1)} %v_hbm.1, bf16[256,128]{1,0:T(8,128)(2,1)} %nk_hbm.1, bf16[256,128]{1,0:T(8,128)(2,1)} %nv_hbm.1, bf16[1024,8192]{1,0:T(8,128)(2,1)} %w_hbm.1, ...), custom_call_target="tpu_custom_call" | custom-call | tf_op jit(solution)/shard_map/pallas_call | solution.py:422
  57.5 1.0 %copy.13 = bf16[256,2048]{1,0:T(8,128)(2,1)} copy(bf16[256,2048]{1,0:T(8,128)(2,1)S(1)} %shard_map.109) | data formatting | bytes 2097152
